TPU v7x, 32 devices: a whole 2x2x4 slice. The times are simulated.
32 devices in a mesh: grp: 2 (over x), bas: 4 (over y, core), aux: 4 (over z).
Axes of the slice: x: 2, y: 2, z: 4, core: 2. Of those that a mesh axis runs over, the one named last changes fastest.
Arguments:
- three_index: bfloat16 [64, 512, 384], P(('grp', 'aux'), 'bas'), parts along dimension 0, may hold values from -6 to 6
- screen: int32 [8, 3], P(('grp', 'bas')), parts along dimension 0, may hold values 0 or 1
- green_occ: bfloat16 [1024, 512], P(('grp', 'bas')), parts along dimension 0, as said below
- green_virt: bfloat16 [1024, 512], P(('grp', 'bas')), parts along dimension 0, as said below
Outputs:
- chi: float32 [64, 32], P(('grp', 'aux'), 'bas'), parts along dimension 0
There are 2 independent parts, one for each index of `grp`. A program takes and returns all parts, laid end to end along the dimension named above; each array names one. Nothing has to cross between parts.
Inputs may be any that keep to these rules, and one draw needn't show every extreme that they name: `green_occ`: symmetric matrix. `green_virt`: symmetric matrix.
All inputs are finite; a program needn't handle non-finite values. No bound on the sum of `screen` on one device may be relied on, other than what follows from the above.
Results may differ from a plain program's by a relative error of at most 0.0041.
Values may be sent and summed in bfloat16 or wider, within the bound.
A program may use at most 128 MiB of HBM per device.

v0:
```python
import math

import jax
import jax.numpy as jnp
from jax import lax
from jax.sharding import PartitionSpec as P


def padded_2(x, sides, width):
    for axis, dim in sides:
        count, length = (lax.axis_size(axis), x.shape[dim])
        up = [(i, (i + 1) % count) for i in range(count)]
        down = [(j, i) for i, j in up]
        last = lax.slice_in_dim(x, length - width, length, axis=dim)
        initial = lax.slice_in_dim(x, 0, width, axis=dim)
        before = lax.ppermute(last, axis, up)
        after = lax.ppermute(initial, axis, down)
        x = jnp.concatenate([before, x, after], axis=dim)
    return x


def body(three_index, screen, green_occ, green_virt):
    width = green_virt.shape[0]
    aux_rows = three_index.shape[0]
    nbasis = green_virt.shape[1]
    screen_flags = screen[0].astype(jnp.bfloat16)
    masked = (
        three_index.reshape(aux_rows, width, 3, width) * screen_flags[None, None, :, None]
    ).reshape(aux_rows, width, 3 * width)
    virt_rows = padded_2(green_virt, (("bas", 0),), width)
    half = jnp.dot(
        masked.reshape(aux_rows * width, 3 * width), virt_rows, preferred_element_type=jnp.float32
    )
    half = half.astype(jnp.bfloat16).reshape(aux_rows, width, nbasis)
    padded = jnp.concatenate([half[:, :, nbasis - width :], half, half[:, :, :width]], 2)

    def one_block(offset):
        begin = offset * width
        occ_cols = lax.dynamic_slice_in_dim(green_occ, begin, width, 1)
        virt_band = lax.dynamic_slice_in_dim(padded, begin, 3 * width, 2)
        return jnp.einsum("lm,alc->mac", occ_cols, virt_band, preferred_element_type=jnp.float32)

    parts_out = lax.map(
        one_block, jnp.arange(lax.axis_size("bas") * width // width, dtype=jnp.int32)
    )
    summed = lax.psum_scatter(
        parts_out.reshape(lax.axis_size("bas") * width, aux_rows, 3 * width),
        "bas",
        scatter_dimension=0,
        tiled=True,
    )
    middle = jnp.transpose(summed, (1, 0, 2)).astype(jnp.bfloat16)
    partial_chi = jnp.einsum(
        "pmc,qmc->pq",
        masked,
        lax.all_gather(middle, "aux", axis=0, tiled=True),
        preferred_element_type=jnp.float32,
    )
    summed_chi = lax.psum_scatter(partial_chi, "bas", scatter_dimension=1, tiled=True)
    return summed_chi * (-2.0 / math.sqrt(3 * width * width))


def solution(mesh):
    in_specs = (
        P(("grp", "aux"), "bas", None),
        P(("grp", "bas"), None),
        P(("grp", "bas"), None),
        P(("grp", "bas"), None),
    )
    out_specs = P(("grp", "aux"), "bas")
    return jax.shard_map(body, mesh=mesh, in_specs=in_specs, out_specs=out_specs, check_vma=False)
```

profile of v0, /device:TPU:0, one launch (start us, length us, event | category | flops | bytes accessed | tf_op | source)
XLA Modules:
  0.0 178.3 jit_solution(5966837182940850723)
XLA Ops:
  7.0 2.0 %collective-permute-start.1 = (bf16[128,512]{1,0:T(8,128)(2,1)}, bf16[128,512]{1,0:T(8,128)(2,1)S(1)}, u32[]{:S(2)}, u32[]{:S(2)}) collective-permute-start(bf16[128,512]{1,0:T(8,128)(2,1)} %param.9), channel_id=1, source_target_pairs={{4,0},{8,4},{12,8},{0,12},{5,1},{9,5},{13,9},{1,13},{6,2},{10,6},{... | collective-permute-start | bytes 393224 | tf_op jit(solution)/shard_map/ppermute | solution.py:17
  8.9 0.7 convert_bitcast_fusion.1
  9.7 1.2 bitcast_multiply_fusion
  10.9 0.9 collective-permute-done
  11.8 1.3 collective-permute-done.1
  13.1 1.6 convolution_convert_fusion
  14.9 1.3 pad_maximum_fusion
  16.2 18.9 %while.10 = (s32[]{:T(128)}, f32[4,128,8,384]{1,2,0,3:T(8,128)}, s32[4]{0:T(128)S(1)}, bf16[128,512]{1,0:T(8,128)(2,1)}, bf16[8,128,768]{2,1,0:T(8,128)(2,1)}, /...) while((s32[]{:T(128)}, f32[4,128,8,384]{1,2,0,3:T(8,128)}, s32[4]{0:T(128)S(1)}, ...), condition=%wide.region_1.2_spmd, body=%wide.region_0.1_spmd.sunk | while | flops 100663304 | bytes 8684224 | solution.py:43
  16.2 0.6 dynamic_slice.21
  17.5 1.5 convolution_bitcast_fusion.3
  19.6 1.3 constant_dynamic-update-slice_fusion.2
  20.9 0.6 dynamic_slice.21
  22.2 1.5 convolution_bitcast_fusion.3
  24.3 1.3 constant_dynamic-update-slice_fusion.2
  26.9 1.5 convolution_bitcast_fusion.3
  29.0 1.3 constant_dynamic-update-slice_fusion.2
  31.6 1.5 convolution_bitcast_fusion.3
  33.8 1.3 constant_dynamic-update-slice_fusion.2
  35.2 60.0 %reduce-scatter.3.cloned.1.call-done = f32[128,8,384]{0,1,2:T(8,128)} async-done(((f32[512,8,384]{0,1,2:T(8,128)}), f32[128,8,384]{0,1,2:T(8,128)}) %reduce-scatter.3.cloned.1.call-update) | async-done | bytes 1572880 | tf_op jit(solution)/shard_map/reduce_scatter | solution.py:46
  95.2 2.4 %convert_bitcast_fusion = bf16[8,128,384]{1,0,2:T(8,128)(2,1)} fusion(f32[128,8,384]{0,1,2:T(8,128)} %reduce-scatter.3.cloned.1.call-done), kind=kLoop, calls=%fused_computation.10 | loop fusion | flops 393216 | bytes 2359296 | tf_op jit(solution)/shard_map/convert_element_type | solution.py:52
  99.5 61.7 %all-gather.2.cloned.1.call-done = bf16[32,128,384]{1,0,2:T(8,128)(2,1)} async-done(((bf16[8,128,384]{1,0,2:T(8,128)(2,1)}), bf16[32,128,384]{1,0,2:T(8,128)(2,1)}) %all-gather.2.cloned.1.call-update) | async-done | bytes 3145744 | tf_op jit(solution)/shard_map/all_gather | solution.py:56
  161.2 2.8 %convolution_bitcast_fusion.1 = f32[8,32]{1,0:T(8,128)S(1)} fusion(bf16[8,128,384]{1,0,2:T(8,128)(2,1)S(1)} %copy.10, bf16[32,128,384]{1,0,2:T(8,128)(2,1)} %all-gather.2.cloned.1.call-done), kind=kOutput, calls=%fused_computation.8 | convolution fusion | flops 25165824 | bytes 3933184 | tf_op jit(solution)/shard_map/pmc,qmc->pq/dot_general | solution.py:53
  164.0 6.8 %all-reduce = f32[8,32]{1,0:T(8,128)S(1)} all-reduce(f32[8,32]{1,0:T(8,128)S(1)} %convolution_bitcast_fusion.1), channel_id=3, replica_groups=mesh['grp'=2,'bas'=4,'aux'=4] {'bas'}, use_global_device_ids=true, to_apply=%region_3.4.clone | all-reduce | flops 256 | bytes 2048
  170.8 0.7 dynamic-slice_multiply_fusion
  (22 shorter events, 5.5 us)
Async XLA Ops:
  6.5 88.7 %reduce-scatter.3.cloned.1.call-start = ((), (), s32[]{:S(2)}) async-start(), calls=%async_computation.1 | async-start | bytes 7864320 | tf_op jit(solution)/shard_map/reduce_scatter | solution.py:46
  6.5 5.3 %collective-permute-start = (bf16[128,512]{1,0:T(8,128)(2,1)}, bf16[128,512]{1,0:T(8,128)(2,1)S(1)}, u32[]{:S(2)}, u32[]{:S(2)}) collective-permute-start(bf16[128,512]{1,0:T(8,128)(2,1)} %param.9), channel_id=1, source_target_pairs={{0,4},{4,8},{8,12},{12,0},{1,5},{5,9},{9,13},{13,1},{2,6},{6,10},{... | collective-permute-start | bytes 393224 | tf_op jit(solution)/shard_map/ppermute | solution.py:16
  7.0 6.1 %collective-permute-start.1 = (bf16[128,512]{1,0:T(8,128)(2,1)}, bf16[128,512]{1,0:T(8,128)(2,1)S(1)}, u32[]{:S(2)}, u32[]{:S(2)}) collective-permute-start(bf16[128,512]{1,0:T(8,128)(2,1)} %param.9), channel_id=1, source_target_pairs={{4,0},{8,4},{12,8},{0,12},{5,1},{9,5},{13,9},{1,13},{6,2},{10,6},{... | collective-permute-start | bytes 393224 | tf_op jit(solution)/shard_map/ppermute | solution.py:17
  35.1 62.5 %copy-start = (bf16[8,128,384]{2,1,0:T(8,128)(2,1)S(1)}, bf16[8,128,384]{2,1,0:T(8,128)(2,1)}, u32[]{:S(2)}) copy-start(bf16[8,128,384]{2,1,0:T(8,128)(2,1)} %param.6) | copy-start | bytes 2359300
  35.1 63.1 %copy-start.1 = (u32[32]{0:T(128)S(1)}, u32[32]{0:T(128)}, u32[]{:S(2)}) copy-start(u32[32]{0:T(128)} %constant.24) | copy-start | bytes 388
  35.2 126.0 %all-gather.2.cloned.1.call-start = ((), (), s32[]{:S(2)}) async-start(), calls=%async_computation.2 | async-start | bytes 3932160 | tf_op jit(solution)/shard_map/all_gather | solution.py:56
Sparse Core Ops, SparseCore 0:
  35.2 59.9 reduce-scatter.2
  97.7 63.3 all-gather.1
where the time goes:
time: 179 us; the launch traced here: 178 us
  waiting for transfers between devices  124 us (69%)
  between operations  14.1 us (8%)
  local copies, waits for them, and re-layouts  11.5 us (6%)
  matrix products  10.6 us (6%)
  blocking collectives  6.83 us (4%)
  other arithmetic  6.29 us (4%)
  loops' own time  2.58 us (1%)
  starting transfers between devices  2.45 us (1%)
    all_gather x1, waiting for transfers between devices, body(): lax.all_gather(middle, 'aux', axis=0, tiled=True)  61.7 us
    reduce_scatter x1, waiting for transfers between devices, body(): lax.psum_scatter(parts_out.reshape(lax.axis_size('bas') * width, aux_rows...  60 us
    dynamic_update_slice x8, local copies, waits for them, and re-layouts, body(): lax.map(one_block, jnp.arange(lax.axis_size('bas') * width // width, dtyp...  7.58 us
    unnamed x1, blocking collectives  6.83 us
    dot_general x4, matrix products, one_block(): jnp.einsum('lm,alc->mac', occ_cols, virt_band, preferred_element_type=jnp...  6.17 us
  transfers between devices with their start and end apart: 4, of which 4 were waited for; matrix products, arithmetic and copies ran while one was open for 2% of the time, Pallas kernels for 0%

commit v1 on v0

--- a/solution.py
+++ b/solution.py
@@ -1,9 +1,299 @@
+import functools
 import math
 
 import jax
 import jax.numpy as jnp
 from jax import lax
+from jax.experimental import pallas as pl
+from jax.experimental.pallas import tpu as pltpu
 from jax.sharding import PartitionSpec as P
+
+MESH = pl.DeviceIdType.MESH
+CHUNKS = 4
+
+
+def kernel(
+    scale,
+    three_ref, screen_ref, occ_ref, virt_ref, out_ref,
+    ball, zall, mid, half, virt_band, virt_ext, part, part_t, chi_in,
+    y_send, y_recv, core_send, core_recv, fwd_send, fwd_recv,
+    virt_send, virt_recv, z_send, z_recv, chi_send, chi_recv,
+):
+    aux_rows, width, band = three_ref.shape
+    blocks = 4
+    step = aux_rows // CHUNKS
+    g, b, z = lax.axis_index("grp"), lax.axis_index("bas"), lax.axis_index("aux")
+    core = b + 1 - 2 * lax.rem(b, 2)
+    across = lax.rem(b + 2, blocks)
+    corner = blocks - 1 - b
+    above, below = lax.rem(b + 1, blocks), lax.rem(b + blocks - 1, blocks)
+
+    barrier = pltpu.get_barrier_semaphore()
+    for k in range(1, 16):
+        other = lax.rem(b * 4 + z + k, 16)
+        pl.semaphore_signal(
+            barrier, inc=1, device_id=(g, other // 4, lax.rem(other, 4)), device_id_type=MESH
+        )
+
+    for w in range(3):
+        flag = jnp.full((width, width), screen_ref[0, w].astype(jnp.float32)).astype(jnp.bfloat16)
+        cols = pl.ds(w * width, width)
+        for q in range(aux_rows):
+            value = three_ref[q, :, cols] * flag
+            ball[b, q, :, cols] = value
+            zall[z, q, :, cols] = value
+    pl.semaphore_wait(barrier, 15)
+
+    def remote(src, dst, send, recv, bas, aux):
+        return pltpu.make_async_remote_copy(
+            src_ref=src, dst_ref=dst, send_sem=send, recv_sem=recv,
+            device_id=(g, bas, aux), device_id_type=MESH,
+        )
+
+    def bas_copy(block, k, sends, recvs, to):
+        rows = ball.at[block, pl.ds(k * step, step)]
+        return remote(rows, rows, sends.at[k], recvs.at[k], to, z)
+
+    def z_copy(source, k, to):
+        rows = zall.at[source, pl.ds(k * step, step)]
+        return remote(rows, rows, z_send.at[source, k], z_recv.at[source, k], b, to)
+
+    z_right, z_left = lax.rem(z + 1, 4), lax.rem(z + 3, 4)
+
+    virt_up = remote(virt_ref, virt_band.at[0], virt_send.at[0], virt_recv.at[0], above, z)
+    virt_down = remote(virt_ref, virt_band.at[2], virt_send.at[1], virt_recv.at[1], below, z)
+    virt_up.start()
+    virt_down.start()
+    for k in range(CHUNKS):
+        bas_copy(b, k, y_send, y_recv, across).start()
+        for s in (0, 1):
+            @pl.when(z == s)
+            def _():
+                z_copy(s, k, z_right).start()
+
+        @pl.when(z == 3)
+        def _():
+            z_copy(3, k, z_left).start()
+        bas_copy(b, k, core_send, core_recv, core).start()
+
+    virt_band[1] = virt_ref[...]
+    virt_up.wait_recv()
+    virt_down.wait_recv()
+    for w in range(3):
+        turned = virt_band[w].astype(jnp.float32).T.astype(jnp.bfloat16)
+        cols = pl.ds(w * width, width)
+        virt_ext[pl.ds(width, blocks * width), cols] = turned
+        virt_ext[pl.ds(0, width), cols] = turned[(blocks - 1) * width :]
+        virt_ext[pl.ds((blocks + 1) * width, width), cols] = turned[:width]
+
+    def middle_of(k):
+        bas_copy(core, k, core_send, core_recv, core).wait_recv()
+        bas_copy(corner, k, fwd_send, fwd_recv, core).wait_recv()
+
+        def one_block(l, carry):
+            rows = pl.ds(pl.multiple_of(l * width, width), width)
+            virt = virt_ext[pl.ds(pl.multiple_of(l * width, width), band), :]
+            three = ball[l, pl.ds(k * step, step)].reshape(step * width, band)
+            value = jnp.dot(three, virt, preferred_element_type=jnp.float32)
+            half[:, rows, :] = value.astype(jnp.bfloat16).reshape(step, width, band)
+            return carry
+
+        lax.fori_loop(0, blocks, one_block, 0)
+        for q in range(step):
+            mid[k * step + q] = jnp.dot(
+                occ_ref[...], half[q], preferred_element_type=jnp.float32
+            ).astype(jnp.bfloat16)
+
+    for k in range(CHUNKS):
+        bas_copy(across, k, y_send, y_recv, across).wait_recv()
+        bas_copy(across, k, fwd_send, fwd_recv, core).start()
+
+        @pl.when(z == 1)
+        def _():
+            z_copy(0, k, z_right).wait_recv()
+            z_copy(0, k, z_right).start()
+
+        @pl.when(z == 2)
+        def _():
+            z_copy(1, k, z_right).wait_recv()
+            z_copy(1, k, z_right).start()
+
+        if k:
+            middle_of(k - 1)
+    middle_of(CHUNKS - 1)
+
+    row = lax.broadcasted_iota(jnp.int32, (width, 2 * width), 0)
+    col = lax.broadcasted_iota(jnp.int32, (width, 2 * width), 1)
+    same = jnp.where((col == row) | (col == row + width), 1.0, 0.0).astype(jnp.float32)
+    lane = lax.broadcasted_iota(jnp.int32, (aux_rows, 128), 1)
+
+    def chi_copy(i, turned):
+        src = part_t.at[i] if turned else part.at[i]
+        return remote(
+            src, chi_in.at[b], chi_send.at[i, int(turned)], chi_recv.at[b],
+            i if turned else z, z if turned else i,
+        )
+
+    def pair(i):
+        def two(t, acc):
+            rows = zall[i].reshape(aux_rows * width, band)
+            ours = mid[pl.ds(2 * t, 2)].reshape(2 * width, band)
+            prod = lax.dot_general(
+                rows, ours, (((1,), (1,)), ((), ())), preferred_element_type=jnp.float32
+            )
+            kept = jnp.sum(prod.reshape(aux_rows, width, 2 * width) * same[None], axis=1)
+            first = jnp.sum(kept[:, :width], axis=1, keepdims=True)
+            second = jnp.sum(kept[:, width:], axis=1, keepdims=True)
+            return jnp.where(lane == 2 * t, first, jnp.where(lane == 2 * t + 1, second, acc))
+
+        acc = lax.fori_loop(0, aux_rows // 2, two, jnp.zeros((aux_rows, 128), jnp.float32))
+        return acc
+
+    def cross(i):
+        acc = pair(i)
+        part[i] = acc
+        full = jnp.concatenate([acc, jnp.zeros((128 - aux_rows, 128), jnp.float32)], 0)
+        part_t[i] = full.T[:aux_rows]
+        chi_copy(i, False).start()
+
+        @pl.when(b == i)
+        def _():
+            chi_in[b] = part_t[i]
+
+        @pl.when(b != i)
+        def _():
+            chi_copy(i, True).start()
+
+    def relay(k):
+        @pl.when(z == 2)
+        def _():
+            z_copy(0, k, z_right).wait_recv()
+            z_copy(0, k, z_right).start()
+
+    relay(0)
+    part[z] = pair(z)
+    own = remote(part.at[z], chi_in.at[b], chi_send.at[z, 0], chi_recv.at[b], z, z)
+
+    @pl.when(b == z)
+    def _():
+        chi_in[b] = part[z]
+
+    @pl.when(b != z)
+    def _():
+        own.start()
+
+    relay(1)
+
+    @pl.when(z >= 2)
+    def _():
+        @pl.when(z == 3)
+        def _():
+            for k in range(CHUNKS):
+                z_copy(1, k, z_right).wait_recv()
+        cross(1)
+
+    relay(2)
+
+    @pl.when(z == 2)
+    def _():
+        for k in range(CHUNKS):
+            z_copy(3, k, z_left).wait_recv()
+        cross(3)
+
+    relay(3)
+
+    @pl.when(z >= 1)
+    def _():
+        @pl.when(z == 3)
+        def _():
+            for k in range(CHUNKS):
+                z_copy(0, k, z_right).wait_recv()
+        cross(0)
+
+    both = jnp.maximum(b, z)
+    least = jnp.minimum(b, z)
+    owner = jnp.where((both == 3) & (least == 2), 2, both)
+    for k in range(blocks):
+        @pl.when((b != k) | (owner != z))
+        def _():
+            remote(part.at[0], chi_in.at[k], chi_send.at[0, 0], chi_recv.at[k], b, z_right).wait_recv()
+    total = chi_in[0] + chi_in[1] + chi_in[2] + chi_in[3]
+    out_ref[...] = total[:, : out_ref.shape[1]] * scale
+
+    virt_up.wait_send()
+    virt_down.wait_send()
+    for k in range(CHUNKS):
+        bas_copy(b, k, y_send, y_recv, across).wait_send()
+        bas_copy(b, k, core_send, core_recv, core).wait_send()
+        bas_copy(across, k, fwd_send, fwd_recv, core).wait_send()
+
+        @pl.when(z <= 2)
+        def _():
+            z_copy(0, k, z_right).wait_send()
+
+        @pl.when((z == 1) | (z == 2))
+        def _():
+            z_copy(1, k, z_right).wait_send()
+
+        @pl.when(z == 3)
+        def _():
+            z_copy(3, k, z_left).wait_send()
+
+    @pl.when(b != z)
+    def _():
+        own.wait_send()
+
+    def cross_sent(i):
+        chi_copy(i, False).wait_send()
+
+        @pl.when(b != i)
+        def _():
+            chi_copy(i, True).wait_send()
+
+    @pl.when(z >= 1)
+    def _():
+        cross_sent(0)
+
+    @pl.when(z >= 2)
+    def _():
+        cross_sent(1)
+
+    @pl.when(z == 2)
+    def _():
+        cross_sent(3)
+
+
+def one_kernel(three_index, screen, green_occ, green_virt):
+    aux_rows, width, band = three_index.shape
+    nbasis = green_virt.shape[1]
+    scale = -2.0 / math.sqrt(3 * width * width)
+    bf16, f32 = jnp.bfloat16, jnp.float32
+    dma = pltpu.SemaphoreType.DMA
+    vmem = pl.BlockSpec(memory_space=pltpu.VMEM)
+    return pl.pallas_call(
+        functools.partial(kernel, scale),
+        out_shape=jax.ShapeDtypeStruct((aux_rows, aux_rows), f32),
+        in_specs=[vmem, pl.BlockSpec(memory_space=pltpu.SMEM), vmem, vmem],
+        out_specs=vmem,
+        scratch_shapes=[
+            pltpu.VMEM((4, aux_rows, width, band), bf16),
+            pltpu.VMEM((4, aux_rows, width, band), bf16),
+            pltpu.VMEM((aux_rows, width, band), bf16),
+            pltpu.VMEM((aux_rows // CHUNKS, nbasis, band), bf16),
+            pltpu.VMEM((3, width, nbasis), bf16),
+            pltpu.VMEM((nbasis + 2 * width, band), bf16),
+            pltpu.VMEM((4, aux_rows, 128), f32),
+            pltpu.VMEM((4, aux_rows, 128), f32),
+            pltpu.VMEM((4, aux_rows, 128), f32),
+        ]
+        + [dma((CHUNKS,))] * 6
+        + [dma((2,))] * 2
+        + [dma((4, CHUNKS))] * 2
+        + [dma((4, 2)), dma((4,))],
+        compiler_params=pltpu.CompilerParams(
+            collective_id=0, has_side_effects=True, vmem_limit_bytes=40 * 1024 * 1024
+        ),
+    )(three_index, screen, green_occ, green_virt)
 
 
 def padded_2(x, sides, width):
@@ -68,4 +358,5 @@
         P(("grp", "bas"), None),
     )
     out_specs = P(("grp", "aux"), "bas")
-    return jax.shard_map(body, mesh=mesh, in_specs=in_specs, out_specs=out_specs, check_vma=False)
+    fits = mesh.shape["bas"] == 4 and mesh.shape["aux"] == 4
+    return jax.shard_map(one_kernel if fits else body, mesh=mesh, in_specs=in_specs, out_specs=out_specs, check_vma=False)

time: 179 us -> 59 us (0.33)
  the two profiles are of different devices: /device:TPU:0 before, /device:TPU:5 now
where the time goes in v1:
time: 59 us; the launch traced here: 58.8 us
  Pallas kernels  54.6 us (93%)
  local copies, waits for them, and re-layouts  4.19 us (7%)
    pallas_call x1, Pallas kernels, one_kernel(): pl.pallas_call(functools.partial(kernel, scale), out_shape=jax.ShapeDtype...  54.6 us
    unnamed x9, local copies, waits for them, and re-layouts  4.19 us

profile of v1, /device:TPU:5, one launch (start us, length us, event | category | flops | bytes accessed | tf_op | source)
XLA Modules:
  0.0 58.8 jit_solution(18174788819888168025)
XLA Ops:
  0.0 0.0 copy-start
  0.0 1.1 %copy-done = bf16[8,128,384]{2,1,0:T(8,128)(2,1)S(1)} copy-done((bf16[8,128,384]{2,1,0:T(8,128)(2,1)S(1)}, bf16[8,128,384]{2,1,0:T(8,128)(2,1)}, u32[]{:S(2)}) %copy-start) | copy-done | bytes 786456
  1.1 0.0 copy-start.1
  1.1 0.9 %copy-done.1 = bf16[128,512]{1,0:T(8,128)(2,1)S(1)} copy-done((bf16[128,512]{1,0:T(8,128)(2,1)S(1)}, bf16[128,512]{1,0:T(8,128)(2,1)}, u32[]{:S(2)}) %copy-start.1) | copy-done | bytes 131096
  2.0 0.0 copy-start.2
  2.0 0.9 %copy-done.2 = bf16[128,512]{1,0:T(8,128)(2,1)S(1)} copy-done((bf16[128,512]{1,0:T(8,128)(2,1)S(1)}, bf16[128,512]{1,0:T(8,128)(2,1)}, u32[]{:S(2)}) %copy-start.2) | copy-done | bytes 131096
  2.9 0.0 copy-start.3
  2.9 0.7 %copy-done.3 = s32[1,3]{1,0:T(1,128)S(1)} copy-done((s32[1,3]{1,0:T(1,128)S(1)}, s32[1,3]{1,0:T(1,128)}, u32[]{:S(2)}) %copy-start.3) | copy-done | bytes 36
  3.6 54.6 %shard_map.46 = f32[8,8]{1,0:T(8,128)S(1)} custom-call(bf16[8,128,384]{2,1,0:T(8,128)(2,1)S(1)} %copy-done, s32[1,3]{1,0:T(1,128)S(1)} %copy-done.3, bf16[128,512]{1,0:T(8,128)(2,1)S(1)} %copy-done.1, bf16[128,512]{1,0:T(8,128)(2,1)S(1)} %copy-done.2), custom_call_target="tpu_custom_call" | custom-call | tf_op jit(solution)/shard_map/pallas_call | solution.py:273
  58.2 0.6 %copy.6 = f32[8,8]{1,0:T(8,128)} copy(f32[8,8]{1,0:T(8,128)S(1)} %shard_map.46) | data formatting | bytes 512
Async XLA Ops:
  0.0 1.1 %copy-start = (bf16[8,128,384]{2,1,0:T(8,128)(2,1)S(1)}, bf16[8,128,384]{2,1,0:T(8,128)(2,1)}, u32[]{:S(2)}) copy-start(bf16[8,128,384]{2,1,0:T(8,128)(2,1)} %three_ref.1) | copy-start | bytes 2359300
  1.1 0.9 %copy-start.1 = (bf16[128,512]{1,0:T(8,128)(2,1)S(1)}, bf16[128,512]{1,0:T(8,128)(2,1)}, u32[]{:S(2)}) copy-start(bf16[128,512]{1,0:T(8,128)(2,1)} %occ_ref.1) | copy-start | bytes 393220
  2.0 0.9 %copy-start.2 = (bf16[128,512]{1,0:T(8,128)(2,1)S(1)}, bf16[128,512]{1,0:T(8,128)(2,1)}, u32[]{:S(2)}) copy-start(bf16[128,512]{1,0:T(8,128)(2,1)} %virt_ref.1) | copy-start | bytes 393220
  2.9 0.7 %copy-start.3 = (s32[1,3]{1,0:T(1,128)S(1)}, s32[1,3]{1,0:T(1,128)}, u32[]{:S(2)}) copy-start(s32[1,3]{1,0:T(1,128)} %screen_ref.1) | copy-start | bytes 40

commit v2 on v1

v2 whole, which is shorter than its diff:
```python
import functools
import math

import jax
import jax.numpy as jnp
from jax import lax
from jax.experimental import pallas as pl
from jax.experimental.pallas import tpu as pltpu
from jax.sharding import PartitionSpec as P

MESH = pl.DeviceIdType.MESH
CHUNKS = 4


def kernel(
    scale,
    three_ref, screen_ref, occ_hbm, virt_hbm, out_ref,
    ball, zall, mall, mid, half, occ_ref, virt_band, virt_ext, flags_ref, part, part_t, chi_in,
    y_send, y_recv, core_send, core_recv, fwd_send, fwd_recv,
    virt_send, virt_recv, z_send, z_recv, chi_send, chi_recv, local_sem,
):
    aux_rows, width, band = three_ref.shape
    blocks = 4
    step = aux_rows // CHUNKS
    late = 3 * width // 8
    early = width - late
    g, b, z = lax.axis_index("grp"), lax.axis_index("bas"), lax.axis_index("aux")
    core = b + 1 - 2 * lax.rem(b, 2)
    across = lax.rem(b + 2, blocks)
    corner = blocks - 1 - b
    above, below = lax.rem(b + 1, blocks), lax.rem(b + blocks - 1, blocks)

    barrier = pltpu.get_barrier_semaphore()
    for k in range(1, 16):
        other = lax.rem(b * 4 + z + k, 16)
        pl.semaphore_signal(
            barrier, inc=1, device_id=(g, other // 4, lax.rem(other, 4)), device_id_type=MESH
        )

    own_copies = [
        pltpu.make_async_copy(screen_ref, flags_ref, local_sem.at[0]),
        pltpu.make_async_copy(three_ref, ball.at[b], local_sem.at[1]),
        pltpu.make_async_copy(virt_hbm, virt_band.at[1], local_sem.at[2]),
        pltpu.make_async_copy(occ_hbm, occ_ref, local_sem.at[3]),
    ]
    for copy in own_copies:
        copy.start()
    own_copies[0].wait()
    own_copies[1].wait()
    lane = lax.broadcasted_iota(jnp.int32, (1, band), 1)
    flags = [flags_ref[0, w].astype(jnp.float32) for w in range(3)]
    flag_row = jnp.where(lane < width, flags[0], jnp.where(lane < 2 * width, flags[1], flags[2]))
    for w in range(3):
        flag = jnp.full((width, width), flags[w]).astype(jnp.bfloat16)
        cols = pl.ds(w * width, width)
        for q in range(aux_rows):
            ball[b, q, :, cols] = ball[b, q, :, cols] * flag
    pl.semaphore_wait(barrier, 15)

    def remote(src, dst, send, recv, bas, aux):
        return pltpu.make_async_remote_copy(
            src_ref=src, dst_ref=dst, send_sem=send, recv_sem=recv,
            device_id=(g, bas, aux), device_id_type=MESH,
        )

    def bas_copy(block, k, sends, recvs, to):
        rows = ball.at[block, pl.ds(k * step, step)]
        return remote(rows, rows, sends.at[k], recvs.at[k], to, z)

    z_right, z_left = lax.rem(z + 1, 4), lax.rem(z + 3, 4)

    def flow(f, k, first):
        aux = pl.ds(k * step, step)
        if f >= 4:
            dst = mall.at[f - 4, aux]
            src = mid.at[aux, pl.ds(early, late)] if first else dst
        else:
            rows = (pl.ds(0, early), pl.ds(0, early), pl.ds(early, late), pl.ds(0, width))[f]
            dst = zall.at[(0, 1, 0, 3)[f], aux, rows]
            src = three_ref.at[aux, rows] if first else dst
        return remote(src, dst, z_send.at[f, k], z_recv.at[f, k], b, z_right if f < 3 else z_left)

    def relay(at, f, k):
        @pl.when(z == at)
        def _():
            flow(f, k, False).wait_recv()
            flow(f, k, False).start()

    def arrived(f):
        for k in range(CHUNKS):
            flow(f, k, False).wait_recv()

    virt_up = remote(virt_hbm, virt_band.at[0], virt_send.at[0], virt_recv.at[0], above, z)
    virt_down = remote(virt_hbm, virt_band.at[2], virt_send.at[1], virt_recv.at[1], below, z)
    for at, f in ((0, 0), (1, 1), (3, 3)):
        @pl.when(z == at)
        def _():
            for k in range(CHUNKS):
                flow(f, k, True).start()
    virt_up.start()
    virt_down.start()
    for k in range(CHUNKS):
        bas_copy(b, k, y_send, y_recv, across).start()
        bas_copy(b, k, core_send, core_recv, core).start()

    @pl.when(z == 0)
    def _():
        for k in range(CHUNKS):
            flow(2, k, True).start()

    own_copies[2].wait()
    own_copies[3].wait()
    virt_up.wait_recv()
    virt_down.wait_recv()
    for w in range(3):
        turned = virt_band[w].astype(jnp.float32).T.astype(jnp.bfloat16)
        cols = pl.ds(w * width, width)
        virt_ext[pl.ds(width, blocks * width), cols] = turned
        virt_ext[pl.ds(0, width), cols] = turned[(blocks - 1) * width :]
        virt_ext[pl.ds((blocks + 1) * width, width), cols] = turned[:width]

    def middle_of(k):
        bas_copy(core, k, core_send, core_recv, core).wait_recv()
        bas_copy(corner, k, fwd_send, fwd_recv, core).wait_recv()

        def one_block(l, carry):
            rows = pl.ds(pl.multiple_of(l * width, width), width)
            virt = virt_ext[pl.ds(pl.multiple_of(l * width, width), band), :]
            three = ball[l, pl.ds(k * step, step)].reshape(step * width, band)
            value = jnp.dot(three, virt, preferred_element_type=jnp.float32)
            half[:, rows, :] = value.astype(jnp.bfloat16).reshape(step, width, band)
            return carry

        lax.fori_loop(0, blocks, one_block, 0)
        for q in range(step):
            value = jnp.dot(occ_ref[...], half[q], preferred_element_type=jnp.float32)
            mid[k * step + q] = (value * flag_row).astype(jnp.bfloat16)
        for at, f in ((2, 4), (3, 5)):
            @pl.when(z == at)
            def _():
                flow(f, k, True).start()

    for k in range(CHUNKS):
        bas_copy(across, k, y_send, y_recv, across).wait_recv()
        bas_copy(across, k, fwd_send, fwd_recv, core).start()
        relay(1, 0, k)
        relay(2, 1, k)
        if k >= 2:
            relay(2, 0, k - 2)
        if k:
            middle_of(k - 1)
        if k >= 2:
            relay(2, 5, k - 2)
            relay(1, 4, k - 2)
        if k >= 3:
            relay(1, 5, k - 3)
    middle_of(CHUNKS - 1)

    chi_lane = lax.broadcasted_iota(jnp.int32, (aux_rows, 128), 1)

    def pair(three, middle):
        count = three.shape[1]
        row = lax.broadcasted_iota(jnp.int32, (count, 2 * count), 0)
        col = lax.broadcasted_iota(jnp.int32, (count, 2 * count), 1)
        same = jnp.where((col == row) | (col == row + count), 1.0, 0.0).astype(jnp.float32)
        left = lax.broadcasted_iota(jnp.int32, (aux_rows, 2 * count), 1) < count

        def two(t, acc):
            rows = three[...].reshape(aux_rows * count, band)
            ours = middle[pl.ds(2 * t, 2)].reshape(2 * count, band)
            prod = lax.dot_general(
                rows, ours, (((1,), (1,)), ((), ())), preferred_element_type=jnp.float32
            )
            kept = jnp.sum(prod.reshape(aux_rows, count, 2 * count) * same[None], axis=1)
            first = jnp.sum(jnp.where(left, kept, 0.0), axis=1, keepdims=True)
            second = jnp.sum(jnp.where(left, 0.0, kept), axis=1, keepdims=True)
            return jnp.where(chi_lane == 2 * t, first, jnp.where(chi_lane == 2 * t + 1, second, acc))

        return lax.fori_loop(0, aux_rows // 2, two, jnp.zeros((aux_rows, 128), jnp.float32))

    def chi_copy(other, turned, slot):
        src = part_t.at[other] if turned else part.at[other]
        to = (z, other) if turned == bool(slot) else (other, z)
        return remote(
            src, chi_in.at[b, slot], chi_send.at[other, int(turned)], chi_recv.at[b, slot], *to
        )

    def share(other, slot, acc):
        part[other] = acc
        full = jnp.concatenate([acc, jnp.zeros((128 - aux_rows, 128), jnp.float32)], 0)
        part_t[other] = full.T[:aux_rows]
        near = slot == 0
        chi_copy(other, not near, slot).start()

        @pl.when(b == other)
        def _():
            chi_in[b, slot] = part_t[other] if near else part[other]

        @pl.when(b != other)
        def _():
            chi_copy(other, near, slot).start()

    relay(2, 0, 2)
    relay(2, 5, 2)
    relay(1, 4, 2)
    relay(1, 5, 1)
    part[z] = pair(ball.at[b], mid)
    own = remote(part.at[z], chi_in.at[b, 0], chi_send.at[z, 0], chi_recv.at[b, 0], z, z)

    @pl.when(b == z)
    def _():
        chi_in[b, 0] = part[z]

    @pl.when(b != z)
    def _():
        own.start()

    relay(2, 0, 3)
    relay(2, 5, 3)
    relay(1, 4, 3)
    relay(1, 5, 2)

    @pl.when(z == 1)
    def _():
        arrived(2)
        share(0, 0, pair(zall.at[0], mid))

    relay(1, 5, 3)

    @pl.when(z == 2)
    def _():
        arrived(3)
        share(3, 0, pair(zall.at[3], mid))

    @pl.when(z >= 2)
    def _():
        for i in (1, 0):
            @pl.when(z == 3)
            def _():
                arrived(i)
            share(i, 0, pair(zall.at[i, :, pl.ds(0, early)], mid.at[:, pl.ds(0, early)]))

    @pl.when(z <= 1)
    def _():
        for i in (2, 3):
            @pl.when(z == 0)
            def _():
                arrived(i + 2)
            share(i, 1, pair(ball.at[b, :, pl.ds(early, late)], mall.at[i - 2]))

    top = jnp.maximum(b, z)
    low = jnp.minimum(b, z)
    owner = jnp.where((top == 3) & (low == 2), 2, top)
    split = (low <= 1) & (top >= 2)

    def chi_arrived(k, slot):
        remote(
            part.at[0], chi_in.at[k, slot], chi_send.at[0, 0], chi_recv.at[k, slot], b, z_right
        ).wait_recv()

    for k in range(blocks):
        @pl.when((b != k) | (owner != z))
        def _():
            chi_arrived(k, 0)

        @pl.when(split & ((b != k) | (low != z)))
        def _():
            chi_arrived(k, 1)
    total = chi_in[0, 0] + chi_in[1, 0] + chi_in[2, 0] + chi_in[3, 0]
    out_ref[...] = total[:, : out_ref.shape[1]] * scale

    @pl.when(split)
    def _():
        rest = chi_in[0, 1] + chi_in[1, 1] + chi_in[2, 1] + chi_in[3, 1]
        out_ref[...] = (total + rest)[:, : out_ref.shape[1]] * scale

    virt_up.wait_send()
    virt_down.wait_send()
    for k in range(CHUNKS):
        bas_copy(b, k, y_send, y_recv, across).wait_send()
        bas_copy(b, k, core_send, core_recv, core).wait_send()
        bas_copy(across, k, fwd_send, fwd_recv, core).wait_send()
    for at, f, first in (
        (0, 0, True), (1, 0, False), (2, 0, False), (1, 1, True), (2, 1, False), (0, 2, True),
        (3, 3, True), (2, 4, True), (1, 4, False), (3, 5, True), (2, 5, False), (1, 5, False),
    ):
        @pl.when(z == at)
        def _():
            for k in range(CHUNKS):
                flow(f, k, first).wait_send()

    @pl.when(b != z)
    def _():
        own.wait_send()

    def shared(other, slot):
        near = slot == 0
        chi_copy(other, not near, slot).wait_send()

        @pl.when(b != other)
        def _():
            chi_copy(other, near, slot).wait_send()

    for at, other, slot in (
        (0, 2, 1), (0, 3, 1), (1, 0, 0), (1, 2, 1), (1, 3, 1),
        (2, 0, 0), (2, 1, 0), (2, 3, 0), (3, 0, 0), (3, 1, 0),
    ):
        @pl.when(z == at)
        def _():
            shared(other, slot)


def one_kernel(three_index, screen, green_occ, green_virt):
    aux_rows, width, band = three_index.shape
    nbasis = green_virt.shape[1]
    scale = -2.0 / math.sqrt(3 * width * width)
    bf16, f32 = jnp.bfloat16, jnp.float32
    dma = pltpu.SemaphoreType.DMA
    return pl.pallas_call(
        functools.partial(kernel, scale),
        out_shape=jax.ShapeDtypeStruct((aux_rows, aux_rows), f32),
        in_specs=[pl.BlockSpec(memory_space=pl.ANY)] * 4,
        out_specs=pl.BlockSpec(memory_space=pltpu.VMEM),
        scratch_shapes=[
            pltpu.VMEM((4, aux_rows, width, band), bf16),
            pltpu.VMEM((4, aux_rows, width, band), bf16),
            pltpu.VMEM((2, aux_rows, 3 * width // 8, band), bf16),
            pltpu.VMEM((aux_rows, width, band), bf16),
            pltpu.VMEM((aux_rows // CHUNKS, nbasis, band), bf16),
            pltpu.VMEM((width, nbasis), bf16),
            pltpu.VMEM((3, width, nbasis), bf16),
            pltpu.VMEM((nbasis + 2 * width, band), bf16),
            pltpu.SMEM((1, 3), jnp.int32),
            pltpu.VMEM((4, aux_rows, 128), f32),
            pltpu.VMEM((4, aux_rows, 128), f32),
            pltpu.VMEM((4, 2, aux_rows, 128), f32),
        ]
        + [dma((CHUNKS,))] * 6
        + [dma((2,))] * 2
        + [dma((6, CHUNKS))] * 2
        + [dma((4, 2)), dma((4, 2)), dma((4,))],
        compiler_params=pltpu.CompilerParams(
            collective_id=0, has_side_effects=True, vmem_limit_bytes=56 * 1024 * 1024
        ),
    )(three_index, screen, green_occ, green_virt)


def padded_2(x, sides, width):
    for axis, dim in sides:
        count, length = (lax.axis_size(axis), x.shape[dim])
        up = [(i, (i + 1) % count) for i in range(count)]
        down = [(j, i) for i, j in up]
        last = lax.slice_in_dim(x, length - width, length, axis=dim)
        initial = lax.slice_in_dim(x, 0, width, axis=dim)
        before = lax.ppermute(last, axis, up)
        after = lax.ppermute(initial, axis, down)
        x = jnp.concatenate([before, x, after], axis=dim)
    return x


def body(three_index, screen, green_occ, green_virt):
    width = green_virt.shape[0]
    aux_rows = three_index.shape[0]
    nbasis = green_virt.shape[1]
    screen_flags = screen[0].astype(jnp.bfloat16)
    masked = (
        three_index.reshape(aux_rows, width, 3, width) * screen_flags[None, None, :, None]
    ).reshape(aux_rows, width, 3 * width)
    virt_rows = padded_2(green_virt, (("bas", 0),), width)
    half = jnp.dot(
        masked.reshape(aux_rows * width, 3 * width), virt_rows, preferred_element_type=jnp.float32
    )
    half = half.astype(jnp.bfloat16).reshape(aux_rows, width, nbasis)
    padded = jnp.concatenate([half[:, :, nbasis - width :], half, half[:, :, :width]], 2)

    def one_block(offset):
        begin = offset * width
        occ_cols = lax.dynamic_slice_in_dim(green_occ, begin, width, 1)
        virt_band = lax.dynamic_slice_in_dim(padded, begin, 3 * width, 2)
        return jnp.einsum("lm,alc->mac", occ_cols, virt_band, preferred_element_type=jnp.float32)

    parts_out = lax.map(
        one_block, jnp.arange(lax.axis_size("bas") * width // width, dtype=jnp.int32)
    )
    summed = lax.psum_scatter(
        parts_out.reshape(lax.axis_size("bas") * width, aux_rows, 3 * width),
        "bas",
        scatter_dimension=0,
        tiled=True,
    )
    middle = jnp.transpose(summed, (1, 0, 2)).astype(jnp.bfloat16)
    partial_chi = jnp.einsum(
        "pmc,qmc->pq",
        masked,
        lax.all_gather(middle, "aux", axis=0, tiled=True),
        preferred_element_type=jnp.float32,
    )
    summed_chi = lax.psum_scatter(partial_chi, "bas", scatter_dimension=1, tiled=True)
    return summed_chi * (-2.0 / math.sqrt(3 * width * width))


def solution(mesh):
    in_specs = (
        P(("grp", "aux"), "bas", None),
        P(("grp", "bas"), None),
        P(("grp", "bas"), None),
        P(("grp", "bas"), None),
    )
    out_specs = P(("grp", "aux"), "bas")
    fits = mesh.shape["bas"] == 4 and mesh.shape["aux"] == 4
    return jax.shard_map(one_kernel if fits else body, mesh=mesh, in_specs=in_specs, out_specs=out_specs, check_vma=False)
```

time: 59 us -> 47.9 us (0.81)
  the two profiles are of different devices: /device:TPU:5 before, /device:TPU:0 now
where the time goes in v2:
time: 47.9 us; the launch traced here: 47.5 us
  Pallas kernels  46.2 us (96%)
  local copies, waits for them, and re-layouts  1.28 us (3%)
    pallas_call x1, Pallas kernels, one_kernel(): pl.pallas_call(functools.partial(kernel, scale), out_shape=jax.ShapeDtype...  46.2 us
    unnamed x1, local copies, waits for them, and re-layouts  1.28 us

profile of v2, /device:TPU:0, one launch (start us, length us, event | category | flops | bytes accessed | tf_op | source)
XLA Modules:
  0.0 47.5 jit_solution(13539952149161559083)
XLA Ops:
  0.0 46.2 %shard_map.46 = f32[8,8]{1,0:T(8,128)} custom-call(bf16[8,128,384]{2,1,0:T(8,128)(2,1)} %three_ref.1, s32[1,3]{1,0:T(1,128)} %screen_ref.1, bf16[128,512]{1,0:T(8,128)(2,1)} %occ_hbm.1, bf16[128,512]{1,0:T(8,128)(2,1)} %virt_hbm.1), custom_call_target="tpu_custom_call" | custom-call | tf_op jit(solution)/shard_map/pallas_call | solution.py:319
  46.2 1.3 %copy.6 = f32[8,8]{1,0:T(8,128)} copy(f32[8,8]{1,0:T(8,128)} %shard_map.46) | data formatting | bytes 512

commit v3 on v2

--- a/solution.py
+++ b/solution.py
@@ -15,9 +15,9 @@
 def kernel(
     scale,
     three_ref, screen_ref, occ_hbm, virt_hbm, out_ref,
-    ball, zall, mall, mid, half, occ_ref, virt_band, virt_ext, flags_ref, part, part_t, chi_in,
+    ball, zall, mall, mid, half, occ_ref, virt_band, virt_ext, flags_ref, flag_rows, part, part_t, chi_in,
     y_send, y_recv, core_send, core_recv, fwd_send, fwd_recv,
-    virt_send, virt_recv, z_send, z_recv, chi_send, chi_recv, local_sem,
+    virt_send, virt_recv, z_send, z_recv, chi_send, chi_recv, flag_send, flag_recv, local_sem,
 ):
     aux_rows, width, band = three_ref.shape
     blocks = 4
@@ -46,15 +46,9 @@
     for copy in own_copies:
         copy.start()
     own_copies[0].wait()
-    own_copies[1].wait()
-    lane = lax.broadcasted_iota(jnp.int32, (1, band), 1)
+    lane = lax.broadcasted_iota(jnp.int32, (8, band), 1)
     flags = [flags_ref[0, w].astype(jnp.float32) for w in range(3)]
-    flag_row = jnp.where(lane < width, flags[0], jnp.where(lane < 2 * width, flags[1], flags[2]))
-    for w in range(3):
-        flag = jnp.full((width, width), flags[w]).astype(jnp.bfloat16)
-        cols = pl.ds(w * width, width)
-        for q in range(aux_rows):
-            ball[b, q, :, cols] = ball[b, q, :, cols] * flag
+    flag_rows[b] = jnp.where(lane < width, flags[0], jnp.where(lane < 2 * width, flags[1], flags[2]))
     pl.semaphore_wait(barrier, 15)
 
     def remote(src, dst, send, recv, bas, aux):
@@ -63,9 +57,10 @@
             device_id=(g, bas, aux), device_id_type=MESH,
         )
 
-    def bas_copy(block, k, sends, recvs, to):
+    def bas_copy(block, k, sends, recvs, to, first=False):
         rows = ball.at[block, pl.ds(k * step, step)]
-        return remote(rows, rows, sends.at[k], recvs.at[k], to, z)
+        src = three_ref.at[pl.ds(k * step, step)] if first else rows
+        return remote(src, rows, sends.at[k], recvs.at[k], to, z)
 
     z_right, z_left = lax.rem(z + 1, 4), lax.rem(z + 3, 4)
 
@@ -99,17 +94,23 @@
                 flow(f, k, True).start()
     virt_up.start()
     virt_down.start()
+    flag_copies = [
+        remote(flag_rows.at[b], flag_rows.at[b], flag_send.at[n], flag_recv.at[n], to, z)
+        for n, to in enumerate((core, across, corner))
+    ]
+    for copy in flag_copies:
+        copy.start()
     for k in range(CHUNKS):
-        bas_copy(b, k, y_send, y_recv, across).start()
-        bas_copy(b, k, core_send, core_recv, core).start()
+        bas_copy(b, k, y_send, y_recv, across, True).start()
+        bas_copy(b, k, core_send, core_recv, core, True).start()
 
     @pl.when(z == 0)
     def _():
         for k in range(CHUNKS):
             flow(2, k, True).start()
 
-    own_copies[2].wait()
-    own_copies[3].wait()
+    for copy in own_copies[1:]:
+        copy.wait()
     virt_up.wait_recv()
     virt_down.wait_recv()
     for w in range(3):
@@ -118,6 +119,37 @@
         virt_ext[pl.ds(width, blocks * width), cols] = turned
         virt_ext[pl.ds(0, width), cols] = turned[(blocks - 1) * width :]
         virt_ext[pl.ds((blocks + 1) * width, width), cols] = turned[:width]
+    for n, sender in enumerate((core, across, corner)):
+        remote(
+            flag_rows.at[b], flag_rows.at[sender], flag_send.at[n], flag_recv.at[n], core, z
+        ).wait_recv()
+    flag_row = flag_rows[b, :1]
+    part[z] = jnp.zeros((aux_rows, 128), jnp.float32)
+
+    chi_lane = lax.broadcasted_iota(jnp.int32, (aux_rows, 128), 1)
+
+    def two_columns(three, middle, t, acc):
+        count = three.shape[1]
+        row = lax.broadcasted_iota(jnp.int32, (count, 2 * count), 0)
+        col = lax.broadcasted_iota(jnp.int32, (count, 2 * count), 1)
+        same = jnp.where((col == row) | (col == row + count), 1.0, 0.0).astype(jnp.float32)
+        left = lax.broadcasted_iota(jnp.int32, (aux_rows, 2 * count), 1) < count
+        rows = three[...].reshape(aux_rows * count, band)
+        ours = middle[pl.ds(2 * t, 2)].reshape(2 * count, band)
+        prod = lax.dot_general(
+            rows, ours, (((1,), (1,)), ((), ())), preferred_element_type=jnp.float32
+        )
+        kept = jnp.sum(prod.reshape(aux_rows, count, 2 * count) * same[None], axis=1)
+        first = jnp.sum(jnp.where(left, kept, 0.0), axis=1, keepdims=True)
+        second = jnp.sum(jnp.where(left, 0.0, kept), axis=1, keepdims=True)
+        return jnp.where(chi_lane == 2 * t, first, jnp.where(chi_lane == 2 * t + 1, second, acc))
+
+    nothing = jnp.zeros((aux_rows, 128), jnp.float32)
+
+    def pair(three, middle):
+        return lax.fori_loop(
+            0, aux_rows // 2, lambda t, acc: two_columns(three, middle, t, acc), nothing
+        )
 
     def middle_of(k):
         bas_copy(core, k, core_send, core_recv, core).wait_recv()
@@ -127,6 +159,7 @@
             rows = pl.ds(pl.multiple_of(l * width, width), width)
             virt = virt_ext[pl.ds(pl.multiple_of(l * width, width), band), :]
             three = ball[l, pl.ds(k * step, step)].reshape(step * width, band)
+            three = three * flag_rows[l, :1].astype(jnp.bfloat16)
             value = jnp.dot(three, virt, preferred_element_type=jnp.float32)
             half[:, rows, :] = value.astype(jnp.bfloat16).reshape(step, width, band)
             return carry
@@ -139,6 +172,10 @@
             @pl.when(z == at)
             def _():
                 flow(f, k, True).start()
+
+    def own_columns(k):
+        for t in range(k * step // 2, (k + 1) * step // 2):
+            part[z] = two_columns(ball.at[b], mid, t, part[z])
 
     for k in range(CHUNKS):
         bas_copy(across, k, y_send, y_recv, across).wait_recv()
@@ -154,29 +191,12 @@
             relay(1, 4, k - 2)
         if k >= 3:
             relay(1, 5, k - 3)
+        if k:
+            own_columns(k - 1)
     middle_of(CHUNKS - 1)
-
-    chi_lane = lax.broadcasted_iota(jnp.int32, (aux_rows, 128), 1)
-
-    def pair(three, middle):
-        count = three.shape[1]
-        row = lax.broadcasted_iota(jnp.int32, (count, 2 * count), 0)
-        col = lax.broadcasted_iota(jnp.int32, (count, 2 * count), 1)
-        same = jnp.where((col == row) | (col == row + count), 1.0, 0.0).astype(jnp.float32)
-        left = lax.broadcasted_iota(jnp.int32, (aux_rows, 2 * count), 1) < count
-
-        def two(t, acc):
-            rows = three[...].reshape(aux_rows * count, band)
-            ours = middle[pl.ds(2 * t, 2)].reshape(2 * count, band)
-            prod = lax.dot_general(
-                rows, ours, (((1,), (1,)), ((), ())), preferred_element_type=jnp.float32
-            )
-            kept = jnp.sum(prod.reshape(aux_rows, count, 2 * count) * same[None], axis=1)
-            first = jnp.sum(jnp.where(left, kept, 0.0), axis=1, keepdims=True)
-            second = jnp.sum(jnp.where(left, 0.0, kept), axis=1, keepdims=True)
-            return jnp.where(chi_lane == 2 * t, first, jnp.where(chi_lane == 2 * t + 1, second, acc))
-
-        return lax.fori_loop(0, aux_rows // 2, two, jnp.zeros((aux_rows, 128), jnp.float32))
+    relay(2, 0, 2)
+    relay(2, 5, 2)
+    own_columns(CHUNKS - 1)
 
     def chi_copy(other, turned, slot):
         src = part_t.at[other] if turned else part.at[other]
@@ -200,11 +220,6 @@
         def _():
             chi_copy(other, near, slot).start()
 
-    relay(2, 0, 2)
-    relay(2, 5, 2)
-    relay(1, 4, 2)
-    relay(1, 5, 1)
-    part[z] = pair(ball.at[b], mid)
     own = remote(part.at[z], chi_in.at[b, 0], chi_send.at[z, 0], chi_recv.at[b, 0], z, z)
 
     @pl.when(b == z)
@@ -216,21 +231,18 @@
         own.start()
 
     relay(2, 0, 3)
-    relay(2, 5, 3)
-    relay(1, 4, 3)
-    relay(1, 5, 2)
 
     @pl.when(z == 1)
     def _():
         arrived(2)
         share(0, 0, pair(zall.at[0], mid))
 
-    relay(1, 5, 3)
-
     @pl.when(z == 2)
     def _():
         arrived(3)
         share(3, 0, pair(zall.at[3], mid))
+
+    relay(2, 5, 3)
 
     @pl.when(z >= 2)
     def _():
@@ -242,11 +254,17 @@
 
     @pl.when(z <= 1)
     def _():
-        for i in (2, 3):
+        acc = {2: nothing, 3: nothing}
+        for i, k in ((2, 0), (2, 1), (3, 0), (2, 2), (3, 1), (2, 3), (3, 2), (3, 3)):
             @pl.when(z == 0)
             def _():
-                arrived(i + 2)
-            share(i, 1, pair(ball.at[b, :, pl.ds(early, late)], mall.at[i - 2]))
+                flow(i + 2, k, False).wait_recv()
+            if (i, k) not in ((2, 0), (2, 1), (3, 0)):
+                relay(1, i + 2, k)
+            for t in range(k * step // 2, (k + 1) * step // 2):
+                acc[i] = two_columns(ball.at[b, :, pl.ds(early, late)], mall.at[i - 2], t, acc[i])
+            if k == CHUNKS - 1:
+                share(i, 1, acc[i])
 
     top = jnp.maximum(b, z)
     low = jnp.minimum(b, z)
@@ -276,9 +294,11 @@
 
     virt_up.wait_send()
     virt_down.wait_send()
+    for copy in flag_copies:
+        copy.wait_send()
     for k in range(CHUNKS):
-        bas_copy(b, k, y_send, y_recv, across).wait_send()
-        bas_copy(b, k, core_send, core_recv, core).wait_send()
+        bas_copy(b, k, y_send, y_recv, across, True).wait_send()
+        bas_copy(b, k, core_send, core_recv, core, True).wait_send()
         bas_copy(across, k, fwd_send, fwd_recv, core).wait_send()
     for at, f, first in (
         (0, 0, True), (1, 0, False), (2, 0, False), (1, 1, True), (2, 1, False), (0, 2, True),
@@ -331,6 +351,7 @@
             pltpu.VMEM((3, width, nbasis), bf16),
             pltpu.VMEM((nbasis + 2 * width, band), bf16),
             pltpu.SMEM((1, 3), jnp.int32),
+            pltpu.VMEM((4, 8, band), f32),
             pltpu.VMEM((4, aux_rows, 128), f32),
             pltpu.VMEM((4, aux_rows, 128), f32),
             pltpu.VMEM((4, 2, aux_rows, 128), f32),
@@ -338,7 +359,7 @@
         + [dma((CHUNKS,))] * 6
         + [dma((2,))] * 2
         + [dma((6, CHUNKS))] * 2
-        + [dma((4, 2)), dma((4, 2)), dma((4,))],
+        + [dma((4, 2)), dma((4, 2)), dma((3,)), dma((3,)), dma((4,))],
         compiler_params=pltpu.CompilerParams(
             collective_id=0, has_side_effects=True, vmem_limit_bytes=56 * 1024 * 1024
         ),

time: 47.9 us -> 49.1 us (1.025)
  Pallas kernels: 46.2 us -> 47.4 us
    pallas_call x1, Pallas kernels: 46.2 us -> 47.4 us  [one_kernel(): pl.pallas_call(functools.partial(kernel, scale), out_shape=jax.ShapeDtype...]
where the time goes in v3:
time: 49.1 us; the launch traced here: 48.7 us
  Pallas kernels  47.4 us (97%)
  local copies, waits for them, and re-layouts  1.28 us (3%)
    pallas_call x1, Pallas kernels, one_kernel(): pl.pallas_call(functools.partial(kernel, scale), out_shape=jax.ShapeDtype...  47.4 us
    unnamed x1, local copies, waits for them, and re-layouts  1.28 us

profile of v3, /device:TPU:0, one launch (start us, length us, event | category | flops | bytes accessed | tf_op | source)
XLA Modules:
  0.0 48.7 jit_solution(15554019612610196633)
XLA Ops:
  0.0 47.4 %shard_map.46 = f32[8,8]{1,0:T(8,128)} custom-call(bf16[8,128,384]{2,1,0:T(8,128)(2,1)} %three_ref.1, s32[1,3]{1,0:T(1,128)} %screen_ref.1, bf16[128,512]{1,0:T(8,128)(2,1)} %occ_hbm.1, bf16[128,512]{1,0:T(8,128)(2,1)} %virt_hbm.1), custom_call_target="tpu_custom_call" | custom-call | tf_op jit(solution)/shard_map/pallas_call | solution.py:339
  47.4 1.3 %copy.6 = f32[8,8]{1,0:T(8,128)} copy(f32[8,8]{1,0:T(8,128)} %shard_map.46) | data formatting | bytes 512

commit v4 on v3

--- a/solution.py
+++ b/solution.py
@@ -73,7 +73,8 @@
             rows = (pl.ds(0, early), pl.ds(0, early), pl.ds(early, late), pl.ds(0, width))[f]
             dst = zall.at[(0, 1, 0, 3)[f], aux, rows]
             src = three_ref.at[aux, rows] if first else dst
-        return remote(src, dst, z_send.at[f, k], z_recv.at[f, k], b, z_right if f < 3 else z_left)
+        to = z_right if f < 3 else lax.rem(z + 2, 4) if f == 5 and first else z_left
+        return remote(src, dst, z_send.at[f, k], z_recv.at[f, k], b, to)
 
     def relay(at, f, k):
         @pl.when(z == at)
@@ -177,25 +178,29 @@
         for t in range(k * step // 2, (k + 1) * step // 2):
             part[z] = two_columns(ball.at[b], mid, t, part[z])
 
+    upward = {
+        1: [(0, k) for k in range(CHUNKS)] + [None] * CHUNKS,
+        2: [(1, k) for k in range(CHUNKS)] + [(0, k) for k in range(CHUNKS)],
+    }
+
+    def pass_up(n):
+        for at, chunks in upward.items():
+            if chunks[n] is not None:
+                relay(at, *chunks[n])
+
     for k in range(CHUNKS):
+        pass_up(2 * k)
         bas_copy(across, k, y_send, y_recv, across).wait_recv()
         bas_copy(across, k, fwd_send, fwd_recv, core).start()
-        relay(1, 0, k)
-        relay(2, 1, k)
-        if k >= 2:
-            relay(2, 0, k - 2)
+        pass_up(2 * k + 1)
         if k:
             middle_of(k - 1)
         if k >= 2:
-            relay(2, 5, k - 2)
             relay(1, 4, k - 2)
-        if k >= 3:
-            relay(1, 5, k - 3)
+            relay(1, 5, k - 2)
         if k:
             own_columns(k - 1)
     middle_of(CHUNKS - 1)
-    relay(2, 0, 2)
-    relay(2, 5, 2)
     own_columns(CHUNKS - 1)
 
     def chi_copy(other, turned, slot):
@@ -230,8 +235,6 @@
     def _():
         own.start()
 
-    relay(2, 0, 3)
-
     @pl.when(z == 1)
     def _():
         arrived(2)
@@ -241,8 +244,6 @@
     def _():
         arrived(3)
         share(3, 0, pair(zall.at[3], mid))
-
-    relay(2, 5, 3)
 
     @pl.when(z >= 2)
     def _():
@@ -255,11 +256,11 @@
     @pl.when(z <= 1)
     def _():
         acc = {2: nothing, 3: nothing}
-        for i, k in ((2, 0), (2, 1), (3, 0), (2, 2), (3, 1), (2, 3), (3, 2), (3, 3)):
+        for i, k in ((2, 0), (3, 0), (2, 1), (3, 1), (2, 2), (3, 2), (2, 3), (3, 3)):
             @pl.when(z == 0)
             def _():
                 flow(i + 2, k, False).wait_recv()
-            if (i, k) not in ((2, 0), (2, 1), (3, 0)):
+            if k >= 2:
                 relay(1, i + 2, k)
             for t in range(k * step // 2, (k + 1) * step // 2):
                 acc[i] = two_columns(ball.at[b, :, pl.ds(early, late)], mall.at[i - 2], t, acc[i])
@@ -302,7 +303,7 @@
         bas_copy(across, k, fwd_send, fwd_recv, core).wait_send()
     for at, f, first in (
         (0, 0, True), (1, 0, False), (2, 0, False), (1, 1, True), (2, 1, False), (0, 2, True),
-        (3, 3, True), (2, 4, True), (1, 4, False), (3, 5, True), (2, 5, False), (1, 5, False),
+        (3, 3, True), (2, 4, True), (1, 4, False), (3, 5, True), (1, 5, False),
     ):
         @pl.when(z == at)
         def _():

time: 49.1 us -> 48 us (0.978)
  Pallas kernels: 47.4 us -> 46.5 us
    pallas_call x1, Pallas kernels: 47.4 us -> 46.5 us  [one_kernel(): pl.pallas_call(functools.partial(kernel, scale), out_shape=jax.ShapeDtype...]
where the time goes in v4:
time: 48 us; the launch traced here: 47.8 us
  Pallas kernels  46.5 us (97%)
  local copies, waits for them, and re-layouts  1.28 us (3%)
    pallas_call x1, Pallas kernels, one_kernel(): pl.pallas_call(functools.partial(kernel, scale), out_shape=jax.ShapeDtype...  46.5 us
    unnamed x1, local copies, waits for them, and re-layouts  1.28 us

profile of v4, /device:TPU:0, one launch (start us, length us, event | category | flops | bytes accessed | tf_op | source)
XLA Modules:
  0.0 47.8 jit_solution(11006188692486718334)
XLA Ops:
  0.0 46.5 %shard_map.46 = f32[8,8]{1,0:T(8,128)} custom-call(bf16[8,128,384]{2,1,0:T(8,128)(2,1)} %three_ref.1, s32[1,3]{1,0:T(1,128)} %screen_ref.1, bf16[128,512]{1,0:T(8,128)(2,1)} %occ_hbm.1, bf16[128,512]{1,0:T(8,128)(2,1)} %virt_hbm.1), custom_call_target="tpu_custom_call" | custom-call | tf_op jit(solution)/shard_map/pallas_call | solution.py:340
  46.5 1.3 %copy.6 = f32[8,8]{1,0:T(8,128)} copy(f32[8,8]{1,0:T(8,128)} %shard_map.46) | data formatting | bytes 512

commit v5 on v4

--- a/solution.py
+++ b/solution.py
@@ -193,15 +193,11 @@
         bas_copy(across, k, y_send, y_recv, across).wait_recv()
         bas_copy(across, k, fwd_send, fwd_recv, core).start()
         pass_up(2 * k + 1)
+        middle_of(k)
         if k:
-            middle_of(k - 1)
-        if k >= 2:
-            relay(1, 4, k - 2)
-            relay(1, 5, k - 2)
-        if k:
-            own_columns(k - 1)
-    middle_of(CHUNKS - 1)
-    own_columns(CHUNKS - 1)
+            relay(1, 4, k - 1)
+            relay(1, 5, k - 1)
+        own_columns(k)
 
     def chi_copy(other, turned, slot):
         src = part_t.at[other] if turned else part.at[other]
@@ -260,7 +256,7 @@
             @pl.when(z == 0)
             def _():
                 flow(i + 2, k, False).wait_recv()
-            if k >= 2:
+            if k == CHUNKS - 1:
                 relay(1, i + 2, k)
             for t in range(k * step // 2, (k + 1) * step // 2):
                 acc[i] = two_columns(ball.at[b, :, pl.ds(early, late)], mall.at[i - 2], t, acc[i])

time: 48 us -> 46.7 us (0.973)
  Pallas kernels: 46.5 us -> 45.2 us
    pallas_call x1, Pallas kernels: 46.5 us -> 45.2 us  [one_kernel(): pl.pallas_call(functools.partial(kernel, scale), out_shape=jax.ShapeDtype...]
where the time goes in v5:
time: 46.7 us; the launch traced here: 46.5 us
  Pallas kernels  45.2 us (97%)
  local copies, waits for them, and re-layouts  1.28 us (3%)
    pallas_call x1, Pallas kernels, one_kernel(): pl.pallas_call(functools.partial(kernel, scale), out_shape=jax.ShapeDtype...  45.2 us
    unnamed x1, local copies, waits for them, and re-layouts  1.28 us

profile of v5, /device:TPU:0, one launch (start us, length us, event | category | flops | bytes accessed | tf_op | source)
XLA Modules:
  0.0 46.5 jit_solution(16835737109458973938)
XLA Ops:
  0.0 45.2 %shard_map.46 = f32[8,8]{1,0:T(8,128)} custom-call(bf16[8,128,384]{2,1,0:T(8,128)(2,1)} %three_ref.1, s32[1,3]{1,0:T(1,128)} %screen_ref.1, bf16[128,512]{1,0:T(8,128)(2,1)} %occ_hbm.1, bf16[128,512]{1,0:T(8,128)(2,1)} %virt_hbm.1), custom_call_target="tpu_custom_call" | custom-call | tf_op jit(solution)/shard_map/pallas_call | solution.py:336
  45.2 1.3 %copy.6 = f32[8,8]{1,0:T(8,128)} copy(f32[8,8]{1,0:T(8,128)} %shard_map.46) | data formatting | bytes 512

commit v6 on v5

--- a/solution.py
+++ b/solution.py
@@ -231,6 +231,9 @@
     def _():
         own.start()
 
+    relay(1, 4, CHUNKS - 1)
+    relay(1, 5, CHUNKS - 1)
+
     @pl.when(z == 1)
     def _():
         arrived(2)
@@ -256,8 +259,6 @@
             @pl.when(z == 0)
             def _():
                 flow(i + 2, k, False).wait_recv()
-            if k == CHUNKS - 1:
-                relay(1, i + 2, k)
             for t in range(k * step // 2, (k + 1) * step // 2):
                 acc[i] = two_columns(ball.at[b, :, pl.ds(early, late)], mall.at[i - 2], t, acc[i])
             if k == CHUNKS - 1:

time: 46.7 us -> 45.3 us (0.970)
  Pallas kernels: 45.2 us -> 43.8 us
    pallas_call x1, Pallas kernels: 45.2 us -> 43.8 us  [one_kernel(): pl.pallas_call(functools.partial(kernel, scale), out_shape=jax.ShapeDtype...]
where the time goes in v6:
time: 45.3 us; the launch traced here: 45.1 us
  Pallas kernels  43.8 us (97%)
  local copies, waits for them, and re-layouts  1.28 us (3%)
    pallas_call x1, Pallas kernels, one_kernel(): pl.pallas_call(functools.partial(kernel, scale), out_shape=jax.ShapeDtype...  43.8 us
    unnamed x1, local copies, waits for them, and re-layouts  1.28 us

profile of v6, /device:TPU:0, one launch (start us, length us, event | category | flops | bytes accessed | tf_op | source)
XLA Modules:
  0.0 45.1 jit_solution(12094043851363911767)
XLA Ops:
  0.0 43.8 %shard_map.46 = f32[8,8]{1,0:T(8,128)} custom-call(bf16[8,128,384]{2,1,0:T(8,128)(2,1)} %three_ref.1, s32[1,3]{1,0:T(1,128)} %screen_ref.1, bf16[128,512]{1,0:T(8,128)(2,1)} %occ_hbm.1, bf16[128,512]{1,0:T(8,128)(2,1)} %virt_hbm.1), custom_call_target="tpu_custom_call" | custom-call | tf_op jit(solution)/shard_map/pallas_call | solution.py:337
  43.8 1.3 %copy.6 = f32[8,8]{1,0:T(8,128)} copy(f32[8,8]{1,0:T(8,128)} %shard_map.46) | data formatting | bytes 512
